TPU v7x, 512 devices: a whole 4x8x8 slice. The times are simulated.
512 devices in a mesh: grp: 16 (over z_lo, x), mem: 32 (over y, z_hi, core).
Axes of the slice: x: 4, y: 8, z: 8 (z_hi: 2, z_lo: 4; z = z_hi * 4 + z_lo), core: 2. Of those that a mesh axis runs over, the one named last changes fastest.
Arguments:
- points: float32 [8192, 128], P(('grp', 'mem')), may hold values from -40 to 40, as said below
- slab: float32 [65536, 128], P('mem'), may hold values from -40 to 40, as said below
Outputs:
- new_points: float32 [8192, 128], P(('grp', 'mem'))
Inputs may be any that keep to these rules, and one draw needn't show every extreme that they name: Support points lie near the chains' centres. `slab`: each block of 2048 rows is one chain with its own centre and scale.
All inputs are finite; a program needn't handle non-finite values.
Results may differ from a plain program's by a relative error of at most 0.0001.
Values sent between devices are 32-bit elements; how exact they have to be, the bound alone decides.
No kernel may reach another device: no remote copies, remote signals or barrier semaphores. Data moves between devices by JAX's collectives and lax.ppermute only.
A program may use at most 64 MiB of HBM per device.

v0:
```python
import jax
import jax.numpy as jnp
from jax import lax
from jax.sharding import PartitionSpec as P


def weights_of(left, right_operand):
    left_square_norm = jnp.sum(jnp.square(left), axis=1)
    right_square_norm = jnp.sum(jnp.square(right_operand), axis=1)
    cross_product = jnp.dot(
        left, right_operand.T, precision=lax.Precision.HIGHEST, preferred_element_type=jnp.float32
    )
    squared_distance = left_square_norm[:, None] + right_square_norm[None, :] - 2.0 * cross_product
    return 1.0 / jnp.sqrt(squared_distance + 1.0)


def pair_terms(anchors, piece):
    wts = weights_of(anchors, piece)
    pair_vec = jnp.dot(
        wts, piece, precision=lax.Precision.HIGHEST, preferred_element_type=jnp.float32
    )
    pair_sum = jnp.sum(wts, axis=1)
    return (pair_vec, pair_sum)


def shards(points, slab):
    owned = points.shape[0]
    width = points.shape[1]
    samp_rows = slab.shape[0]
    groups = lax.axis_size("grp")
    ratio = samp_rows / (owned * groups)
    group = lax.all_gather(points, "mem", axis=0, tiled=True)
    sblock = min(samp_rows, 512)
    slab_blocks = slab.reshape(samp_rows // sblock, sblock, width)

    def attract_step(carry, rows):
        numer, total = carry
        wts = weights_of(group, rows)
        numer = numer + jnp.dot(
            wts, rows, precision=lax.Precision.HIGHEST, preferred_element_type=jnp.float32
        )
        total = total + jnp.sum(wts, axis=1)
        return ((numer, total), None)

    init = (
        jnp.zeros((group.shape[0], width), jnp.float32),
        jnp.zeros((group.shape[0],), jnp.float32),
    )
    (numer, total), _ = lax.scan(attract_step, init, slab_blocks)
    numer_all, total_all = lax.psum((numer, total), "mem")
    first = lax.axis_index("mem") * owned
    numer_own = lax.dynamic_slice_in_dim(numer_all, first, owned, 0)
    total_own = lax.dynamic_slice_in_dim(total_all, first, owned, 0)
    pair_vec, pair_sum = pair_terms(
        points, lax.all_gather(points, ("grp", "mem"), axis=0, tiled=True)
    )
    repel = points * pair_sum[:, None] - pair_vec
    update_output = (ratio * repel + numer_own) / total_own[:, None]
    return update_output


def solution(mesh):
    placed = (P(("grp", "mem"), None), P("mem", None))
    return jax.shard_map(
        shards, mesh=mesh, in_specs=placed, out_specs=P(("grp", "mem"), None), check_vma=False
    )
```

profile of v0, /device:TPU:8, one launch (start us, length us, event | category | flops | bytes accessed | tf_op | source)
XLA Modules:
  0.0 842.3 jit_solution(9507223085409808582)
XLA Ops:
  7.4 0.0 all-gather.2.cloned.1.call-start
  7.4 0.7 all-gather.2.cloned.1.call-update
  8.1 0.0 all-reduce.2.cloned.1.call-start
  8.2 57.0 %all_gather.7 = f32[512,128]{1,0:T(8,128)S(1)} all-gather(f32[16,128]{1,0:T(8,128)} %param.4), channel_id=1, replica_groups=mesh['grp'=16,'mem'=32] {'mem'}, dimensions={0}, use_global_device_ids=true | all-gather | bytes 270336 | tf_op jit(solution)/shard_map/all_gather | solution.py:32
  65.2 0.1 multiply_reduce_fusion.1
  65.3 0.0 copy-start.2
  65.3 24.2 %while.15 = (s32[]{:T(128)}, f32[512,128]{1,0:T(8,128)S(1)}, f32[512]{0:T(512)S(1)}, f32[512]{0:T(512)S(1)}, f32[4,512,128]{2,1,0:T(8,128)}, /*index=5*/f32[512,128]{1,0:T(8,128)S(1)}, s32[]{:T(128)}, s32[]{:T(128)}) while((s32[]{:T(128)}, f32[512,128]{1,0:T(8,128)S(1)}, f32[512]{0:T(512)S(1)}, f32[512]{0:T(512)S(1)}, ...), condition=%wide.region_7.8_spmd.clone, body=%wide.region_4.7_spmd.clone.sunk | while | flops 806879232 | bytes 3685476 | solution.py:49
  65.3 1.1 fusion.33
  66.4 2.1 fusion.34
  68.5 2.8 convolution_add_fusion.2
  71.4 1.1 fusion.33
  72.5 2.1 fusion.34
  74.6 2.8 convolution_add_fusion.2
  77.4 1.1 fusion.33
  78.5 2.1 fusion.34
  80.6 2.8 convolution_add_fusion.2
  83.5 1.1 fusion.33
  84.6 2.1 fusion.34
  86.7 2.8 convolution_add_fusion.2
  89.5 0.0 copy-start.1
  89.5 0.7 copy-done.1
  90.2 0.0 all-reduce.2.cloned.1.call-update
  90.2 0.0 copy-done.2
  90.2 0.1 multiply_reduce_fusion.2
  90.4 76.3 %psum.15 = f32[512]{0:T(512)S(1)} all-reduce(f32[512]{0:T(512)S(1)} %get-tuple-element.73), channel_id=1, replica_groups=mesh['grp'=16,'mem'=32] {'mem'}, use_global_device_ids=true, to_apply=%region_9.10 | all-reduce | flops 512 | bytes 4096 | tf_op jit(solution)/shard_map/psum | solution.py:50
  166.6 0.1 dynamic_slice.13
  166.7 656.5 %all-gather.2.cloned.1.call-done = f32[8192,128]{1,0:T(8,128)} async-done(((f32[16,128]{1,0:T(8,128)}), f32[8192,128]{1,0:T(8,128)}) %all-gather.2.cloned.1.call-update) | async-done | bytes 4194320 | tf_op jit(solution)/shard_map/all_gather | solution.py:55
  823.2 3.5 multiply_reduce_fusion
  826.7 0.0 copy-done
  826.7 3.6 fusion.18
  830.3 0.0 all-reduce.2.cloned.1.call-done
  830.4 4.5 fusion.16
  (7 shorter events, 0.1 us)
Async XLA Ops:
  7.4 815.8 %all-gather.2.cloned.1.call-start = ((), (), s32[]{:S(2)}) async-start(), calls=%async_computation | async-start | bytes 4202496 | tf_op jit(solution)/shard_map/all_gather | solution.py:55
  8.1 822.3 %all-reduce.2.cloned.1.call-start = ((), (), s32[]{:S(2)}) async-start(), calls=%async_computation.1 | async-start | bytes 524288 | tf_op jit(solution)/shard_map/psum | solution.py:50
  65.3 24.9 %copy-start.2 = (f32[16,128]{1,0:T(8,128)S(1)}, f32[16,128]{1,0:T(8,128)}, u32[]{:S(2)}) copy-start(f32[16,128]{1,0:T(8,128)} %param.4) | copy-start | bytes 24580
  89.5 0.7 copy-start.1
  823.2 3.5 copy-start
Sparse Core Ops, SparseCore 0:
  10.4 812.7 all-gather.1
Sparse Core Ops, SparseCore 1:
  90.3 330.8 all-reduce.1
where the time goes:
time: 843 us; the launch traced here: 842 us
  waiting for transfers between devices  657 us (78%)
  blocking collectives  133 us (16%)
  matrix products  27.8 us (3%)
  between operations  14.9 us (2%)
    all_gather x1, waiting for transfers between devices, shards(): lax.all_gather(points, ('grp', 'mem'), axis=0, tiled=True)  656 us
    psum x1, blocking collectives, shards(): numer_all, total_all = lax.psum((numer, total), 'mem')  76.3 us
    all_gather x1, blocking collectives, shards(): group = lax.all_gather(points, 'mem', axis=0, tiled=True)  57 us
  transfers between devices with their start and end apart: 2, of which 1 were waited for; matrix products, arithmetic and copies ran while one was open for 4% of the time, Pallas kernels for 0%

commit v1 on v0

--- a/solution.py
+++ b/solution.py
@@ -52,7 +52,13 @@
     numer_own = lax.dynamic_slice_in_dim(numer_all, first, owned, 0)
     total_own = lax.dynamic_slice_in_dim(total_all, first, owned, 0)
     pair_vec, pair_sum = pair_terms(
-        points, lax.all_gather(points, ("grp", "mem"), axis=0, tiled=True)
+        points,
+        jnp.concatenate(
+            lax.all_to_all(
+                jnp.stack([points] * lax.axis_size(("grp", "mem"))), ("grp", "mem"), 0, 0
+            ),
+            axis=0,
+        ),
     )
     repel = points * pair_sum[:, None] - pair_vec
     update_output = (ratio * repel + numer_own) / total_own[:, None]

time: 843 us -> 532 us (0.63)
  the two profiles are of different devices: /device:TPU:8 before, /device:TPU:1 now
where the time goes in v1:
time: 532 us; the launch traced here: 531 us
  waiting for transfers between devices  249 us (47%)
  blocking collectives  214 us (40%)
  starting transfers between devices  24.3 us (5%)
  matrix products  21.9 us (4%)
  between operations  13.5 us (3%)
    psum x1, waiting for transfers between devices, shards(): numer_all, total_all = lax.psum((numer, total), 'mem')  249 us
    all_gather x1, blocking collectives, shards(): group = lax.all_gather(points, 'mem', axis=0, tiled=True)  130 us
    psum x1, blocking collectives, shards(): numer_all, total_all = lax.psum((numer, total), 'mem')  84 us
    all_to_all x1, starting transfers between devices, shards(): lax.all_to_all(jnp.stack([points] * lax.axis_size(('grp', 'mem'))), ('grp...  24.2 us
  transfers between devices with their start and end apart: 2, of which 1 were waited for; matrix products, arithmetic and copies ran while one was open for 4% of the time, Pallas kernels for 0%

profile of v1, /device:TPU:1, one launch (start us, length us, event | category | flops | bytes accessed | tf_op | source)
XLA Modules:
  0.0 531.3 jit_solution(17945547349716435772)
XLA Ops:
  6.5 2.9 stack.2
  9.5 24.2 %all-to-all-start = ((f32[512,16,128]{2,1,0:T(8,128)}), f32[512,16,128]{2,1,0:T(8,128)}, u32[]{:S(2)}, u32[]{:S(2)}) async-start(f32[512,16,128]{2,1,0:T(8,128)} %stack.2), calls=%async_computation | async-start | bytes 8388608 | tf_op jit(solution)/shard_map/all_to_all | solution.py:57
  33.7 0.0 all-reduce.2.cloned.1.call-start
  33.8 0.0 copy-done.2
  33.8 130.3 %all_gather.3 = f32[512,128]{1,0:T(8,128)S(1)} all-gather(f32[16,128]{1,0:T(8,128)S(1)} %copy-done.2), channel_id=1, replica_groups=mesh['grp'=16,'mem'=32] {'mem'}, dimensions={0}, use_global_device_ids=true | all-gather | bytes 270336 | tf_op jit(solution)/shard_map/all_gather | solution.py:32
  164.1 0.1 multiply_reduce_fusion.1
  164.2 0.0 copy-done
  164.2 12.8 %while.15 = (s32[]{:T(128)}, f32[512,128]{1,0:T(8,128)S(1)}, f32[512]{0:T(512)S(1)}, f32[512]{0:T(512)S(1)}, f32[4,512,128]{2,1,0:T(8,128)S(1)}, /*index=5*/f32[512,128]{1,0:T(8,128)S(1)}, s32[]{:T(128)}, s32[]{:T(128)}) while((s32[]{:T(128)}, f32[512,128]{1,0:T(8,128)S(1)}, f32[512]{0:T(512)S(1)}, f32[512]{0:T(512)S(1)}, ...), condition=%wide.region_7.8_spmd.clone, body=%wide.region_4.7_spmd.clone.sunk | while | flops 806879232 | bytes 3684468 | solution.py:49
  164.3 0.2 fusion.33
  164.4 1.2 fusion.34
  165.6 1.8 convolution_add_fusion.2
  167.5 0.2 fusion.33
  167.6 1.2 fusion.34
  168.8 1.8 convolution_add_fusion.2
  170.7 0.2 fusion.33
  170.8 1.2 fusion.34
  172.0 1.8 convolution_add_fusion.2
  173.9 0.2 fusion.33
  174.0 1.2 fusion.34
  175.2 1.8 convolution_add_fusion.2
  177.0 0.0 copy-start.1
  177.1 0.7 copy-done.1
  177.7 0.0 all-reduce.2.cloned.1.call-update
  177.8 84.0 %psum.15 = f32[512]{0:T(512)S(1)} all-reduce(f32[512]{0:T(512)S(1)} %get-tuple-element.73), channel_id=1, replica_groups=mesh['grp'=16,'mem'=32] {'mem'}, use_global_device_ids=true, to_apply=%region_9.10 | all-reduce | flops 512 | bytes 4096 | tf_op jit(solution)/shard_map/psum | solution.py:50
  261.8 0.1 dynamic_slice.13
  261.8 0.1 multiply_reduce_fusion.2
  261.9 0.0 all-to-all-done
  261.9 3.4 multiply_reduce_fusion
  265.3 0.1 add.69
  265.4 5.4 %fusion.18 = (f32[16]{0:T(128)S(1)}, f32[16,8192]{1,0:T(8,128)S(1)}) fusion(f32[16,128]{1,0:T(8,128)S(1)} %copy-done.2, f32[8192,128]{1,0:T(8,128)} %bitcast, f32[8192]{0:T(1024)S(1)} %add.69, f32[16]{0:T(128)S(1)} %multiply_reduce_fusion.2), kind=kOutput, calls=%fused_computation.27 | convolution fusion | flops 201981936 | bytes 4759680 | tf_op jit(solution)/shard_map/dot_general | solution.py:10
  270.9 249.0 %all-reduce.2.cloned.1.call-done = f32[512,128]{1,0:T(8,128)} async-done(((f32[512,128]{1,0:T(8,128)}), f32[512,128]{1,0:T(8,128)}) %all-reduce.2.cloned.1.call-update) | async-done | bytes 262160 | tf_op jit(solution)/shard_map/psum | solution.py:50
  519.9 4.5 fusion.16
  (8 shorter events, 0.1 us)
Async XLA Ops:
  9.5 24.3 %copy-start.2 = (f32[16,128]{1,0:T(8,128)S(1)}, f32[16,128]{1,0:T(8,128)}, u32[]{:S(2)}) copy-start(f32[16,128]{1,0:T(8,128)} %param.4) | copy-start | bytes 24580
  9.5 154.8 %copy-start = (f32[2048,128]{1,0:T(8,128)S(1)}, f32[2048,128]{1,0:T(8,128)}, u32[]{:S(2)}) copy-start(f32[2048,128]{1,0:T(8,128)} %param.5) | copy-start | bytes 3145732
  9.5 252.5 %all-to-all-start = ((f32[512,16,128]{2,1,0:T(8,128)}), f32[512,16,128]{2,1,0:T(8,128)}, u32[]{:S(2)}, u32[]{:S(2)}) async-start(f32[512,16,128]{2,1,0:T(8,128)} %stack.2), calls=%async_computation | async-start | bytes 8388608 | tf_op jit(solution)/shard_map/all_to_all | solution.py:57
  33.7 486.2 %all-reduce.2.cloned.1.call-start = ((), (), s32[]{:S(2)}) async-start(), calls=%async_computation.1 | async-start | bytes 524288 | tf_op jit(solution)/shard_map/psum | solution.py:50
  177.0 0.7 copy-start.1
Sparse Core Ops, SparseCore 0:
  177.9 341.9 all-reduce.1
